TPU v7x, 32 devices: a whole 2x2x4 slice. The times are simulated.
32 devices in a mesh: row: 16 (over z, x, core), col: 2 (over y).
Axes of the slice: x: 2, y: 2, z: 4, core: 2. Of those that a mesh axis runs over, the one named last changes fastest.
Arguments:
- features: bfloat16 [128, 32768], P(None, 'row'), may hold values from -6 to 6
- weight_in: bfloat16 [128, 512], P(None, 'col'), may hold values from -0.5 to 0.5
- weight_out: bfloat16 [512, 64], replicated, may hold values from -0.25 to 0.25
- score_grad: bfloat16 [64, 32768], P('col', 'row'), may hold values from -0.011962891 to 0.011962891
- band_blocks: bfloat16 [256, 3, 128, 128], P('row'), may hold values from -0.25 to 0.25
- long_blocks: bfloat16 [192, 128, 128], P('row'), may hold values from -0.25 to 0.25
- long_rows: int32 [16, 12], P('row'), may hold values from 0 to 15
- long_sources: int32 [16, 12], replicated, may hold values from 0 to 255, as said below
- long_counts: int32 [16], replicated, may hold values from 1 to 12, as said below
Outputs:
- scores: bfloat16 [64, 32768], P('col', 'row')
- first_grad: float32 [128, 512], P(None, 'col')
- second_grad: float32 [512, 64], P('col')
Inputs may be any that keep to these rules, and one draw needn't show every extreme that they name: `long_sources`: every slot's block column lies on a partition at cycle distance 1 to 3 from the slot's own partition (either direction, indices taken mod the number of partitions); over ALL 12 slots of a partition each of the 6 such partitions is read by exactly 2 slots. Slots s < long_counts[p] are live, the others are ignored; some partition has all 12 live.
All inputs are finite; a program needn't handle non-finite values.
Results may differ from a plain program's by a relative error of at most 0.0065.
Values may be sent and summed in bfloat16 or wider, within the bound.
A program may use at most 128 MiB of HBM per device.

v0:
```python
import functools

import jax
import jax.numpy as jnp
from jax import lax
from jax.experimental import pallas as pl
from jax.experimental.pallas import tpu as pltpu
from jax.sharding import PartitionSpec as P

BLK = 128
SLOTS = 12
VMEM_BYTES = 60 * 1024 * 1024
DISTANCES = (-3, -2, -1, 1, 2, 3)
BEFORE = DISTANCES.index(-1)
BEYOND = DISTANCES.index(1)
NEAR_FIRST = sorted(range(6), key=lambda pos: abs(DISTANCES[pos]))
MESH = pl.DeviceIdType.MESH
F32 = jnp.float32
BF16 = jnp.bfloat16


def nn(a, b):
    return lax.dot_general(a, b, (((1,), (0,)), ((), ())), preferred_element_type=F32)


def nt(a, b):
    return lax.dot_general(a, b, (((1,), (1,)), ((), ())), preferred_element_type=F32)


def lanes(block):
    if isinstance(block, int):
        return pl.ds(block * BLK, BLK)
    return pl.ds(pl.multiple_of(block * BLK, BLK), BLK)


def blocks_sent(pos):
    return 3 if pos in (BEFORE, BEYOND) else 2


def kernel(
    rows_n, cols_n, reduce_here,
    x_hbm, win_hbm, wout_hbm, sg_hbm, band_hbm, long_hbm, rows_hbm, src_hbm, count_hbm,
    scores_hbm, first_hbm, second_hbm,
    scores_ref, first_ref, second_ref, out_sem,
    x_ref, win_ref, wout_ref, sg_ref, band_ref, long_ref, rows_ref, src_ref, count_ref, in_sem,
    xb, sb, xs, xr, gs, gr, cs, cr, zacc, contrib, z, gacc, g2, part, part_out, part_in, cls, red, red_in, summed,
    x_ss, x_rs, g_ss, g_rs, c_ss, c_rs, gc_ss, gc_rs, p_ss, p_rs, red_ss, red_rs, all_ss, all_rs,
):
    me = lax.axis_index("row")
    mc = lax.axis_index("col")
    nodes = x_ref.shape[1]
    nb = nodes // BLK
    hidden = win_ref.shape[1]
    cc = sg_ref.shape[0]
    wire = gs.dtype

    operands = [
        pltpu.make_async_copy(src, dst, in_sem.at[i])
        for i, (src, dst) in enumerate((
            (rows_hbm, rows_ref), (src_hbm, src_ref), (count_hbm, count_ref), (sg_hbm, sg_ref), (long_hbm, long_ref),
            (x_hbm, x_ref), (band_hbm, band_ref), (win_hbm, win_ref), (wout_hbm, wout_ref),
        ))
    ]
    for copy in operands:
        copy.start()

    def row_at(by):
        return lax.rem(me + (by + rows_n), rows_n)

    def col_at(by):
        return lax.rem(mc + by, cols_n)

    barrier = pltpu.get_barrier_semaphore()
    if reduce_here:
        def greet(k, carry):
            pl.semaphore_signal(barrier, inc=1, device_id={"row": row_at(k)}, device_id_type=MESH)
            return carry
        lax.fori_loop(1, rows_n, greet, 0, unroll=5)
        expected = rows_n - 1
    else:
        for d in DISTANCES:
            pl.semaphore_signal(barrier, inc=1, device_id={"row": row_at(d)}, device_id_type=MESH)
        expected = len(DISTANCES)
    for k in range(1, cols_n):
        pl.semaphore_signal(barrier, inc=1, device_id={"col": col_at(k)}, device_id_type=MESH)
    expected += cols_n - 1

    def slots_of(owners, owner):
        low, high = jnp.int32(0), jnp.int32(0)
        for s in range(SLOTS):
            high = jnp.where(owners[s] == owner, s, high)
            low = jnp.where(owners[SLOTS - 1 - s] == owner, SLOTS - 1 - s, low)
        return low, high

    def owners_of(reader):
        return [lax.div(src_ref[reader, s], nb) for s in range(SLOTS)]

    for copy in operands[:3]:
        copy.wait()
    my_owners = owners_of(me)
    served, read = [], []
    for d in DISTANCES:
        reader = row_at(-d)
        served.append([
            jnp.clip(src_ref[reader, s] - me * nb, 0, nb - 1) for s in slots_of(owners_of(reader), me)
        ])
        read.append([
            (s, jnp.clip(rows_ref[0, s], 0, nb - 1), (s < count_ref[me]).astype(F32))
            for s in slots_of(my_owners, row_at(d))
        ])

    for copy in operands[3:5]:
        copy.wait()
    for r in range(nb):
        sb[r] = sg_ref[:, lanes(r)].astype(wire)
    for pos in range(6):
        for rank in range(2):
            s, row, live = read[pos][rank]
            gs[pos, rank] = (live * nn(sb[row].astype(BF16), long_ref[s])).astype(wire)
    for copy in operands[5:7]:
        copy.wait()
    gs[BEFORE, 2] = nn(sg_ref[:, lanes(0)], band_ref[0, 0]).astype(wire)
    gs[BEYOND, 2] = nn(sg_ref[:, lanes(nb - 1)], band_ref[nb - 1, 2]).astype(wire)
    for r in range(nb):
        xb[r] = x_ref[:, lanes(r)]
    for pos in range(6):
        for rank in range(2):
            xs[pos, rank] = xb[served[pos][rank]]
    xs[BEFORE, 2] = xb[nb - 1]
    xs[BEYOND, 2] = xb[0]

    pl.semaphore_wait(barrier, expected)

    def swap(src, dst, ss, rs, pos, to):
        span = pl.ds(0, blocks_sent(pos))
        return pltpu.make_async_remote_copy(
            src_ref=src.at[pos, span], dst_ref=dst.at[pos, span],
            send_sem=ss.at[pos], recv_sem=rs.at[pos],
            device_id={"row": to}, device_id_type=MESH,
        )

    g_copies = [swap(gs, gr, g_ss, g_rs, pos, row_at(d)) for pos, d in enumerate(DISTANCES)]
    x_copies = [swap(xs, xr, x_ss, x_rs, pos, row_at(-d)) for pos, d in enumerate(DISTANCES)]
    for copies in (g_copies, x_copies):
        for pos in reversed(NEAR_FIRST):
            copies[pos].start()

    def three(r):
        start = (r - 1) * BLK
        return pl.ds(start if isinstance(r, int) else pl.multiple_of(start, BLK), 3 * BLK)

    def inner(body):
        lax.fori_loop(1, nb - 1, lambda r, c: (body(r), c)[1], 0, unroll=7)

    def g_band(r):
        blocks = jnp.concatenate([band_ref[r - 1, 2], band_ref[r, 1], band_ref[r + 1, 0]], 0)
        gacc[r] = nn(sg_ref[:, three(r)], blocks)

    def z_band(r):
        blocks = jnp.concatenate([band_ref[r, 0], band_ref[r, 1], band_ref[r, 2]], 1)
        zacc[r] = nt(x_ref[:, three(r)], blocks)

    last = nb - 1
    inner(g_band)
    gacc[0] = nn(sg_ref[:, lanes(0)], band_ref[0, 1]) + nn(sg_ref[:, lanes(1)], band_ref[1, 0])
    gacc[last] = nn(sg_ref[:, lanes(last)], band_ref[last, 1]) + nn(sg_ref[:, lanes(last - 1)], band_ref[last - 1, 2])

    for copy in g_copies:
        copy.wait_recv()
    gacc[0] += gr[BEYOND, 2].astype(F32)
    gacc[nb - 1] += gr[BEFORE, 2].astype(F32)

    def g_long(r, carry):
        total = gacc[r]
        for pos in range(6):
            for rank in range(2):
                total += (served[pos][rank] == r).astype(F32) * gr[pos, rank].astype(F32)
        g2[mc, :, lanes(r)] = total.astype(BF16).astype(wire)
        return carry

    lax.fori_loop(0, nb, g_long, 0, unroll=4)

    def g_share(k):
        return pltpu.make_async_remote_copy(
            src_ref=g2.at[mc], dst_ref=g2.at[mc],
            send_sem=gc_ss.at[k - 1], recv_sem=gc_rs.at[k - 1],
            device_id={"col": col_at(k)}, device_id_type=MESH,
        )

    def g_arrives(k):
        return pltpu.make_async_remote_copy(
            src_ref=g2.at[mc], dst_ref=g2.at[col_at(cols_n - k)],
            send_sem=gc_ss.at[k - 1], recv_sem=gc_rs.at[k - 1],
            device_id={"col": col_at(k)}, device_id_type=MESH,
        )

    g_shares = [g_share(k) for k in range(1, cols_n)]
    for copy in g_shares:
        copy.start()

    inner(z_band)
    zacc[0] = nt(xb[0], band_ref[0, 1]) + nt(xb[1], band_ref[0, 2])
    zacc[last] = nt(xb[last - 1], band_ref[last, 0]) + nt(xb[last], band_ref[last, 1])

    for copy in operands[7:]:
        copy.wait()
    win_t = win_ref[...].astype(F32).T.astype(BF16)
    out_f = jnp.zeros((wout_ref.shape[0], hidden), F32)
    for c in range(cols_n):
        out_f += (mc == c).astype(F32) * wout_ref[:, c * hidden:(c + 1) * hidden].astype(F32)
    out_t = out_f.astype(BF16)
    my_out = out_f.T.astype(BF16)
    first_ref[...] = jnp.zeros_like(first_ref)
    second_ref[...] = jnp.zeros_like(second_ref)

    for pos in NEAR_FIRST:
        x_copies[pos].wait_recv()
        for rank in range(2):
            contrib[rank] = nt(xr[pos, rank], long_ref[read[pos][rank][0]])
        if pos == BEFORE:
            zacc[0] += nt(xr[pos, 2], band_ref[0, 0])
        if pos == BEYOND:
            zacc[last] += nt(xr[pos, 2], band_ref[last, 2])

        def z_long(r, carry, pos=pos):
            total = zacc[r]
            for rank in range(2):
                s, row, live = read[pos][rank]
                total += (live * (row == r).astype(F32)) * contrib[rank]
            if pos == NEAR_FIRST[-1]:
                z[:, lanes(r)] = total.astype(BF16)
            else:
                zacc[r] = total
            return carry

        lax.fori_loop(0, nb, z_long, 0, unroll=4)

    tile = 4 * BLK
    tiles = nodes // tile

    def tile_at(t):
        return pl.ds(t * tile, tile)

    def p_share(k, t):
        return pltpu.make_async_remote_copy(
            src_ref=part_out.at[col_at(k), :, tile_at(t)], dst_ref=part_in.at[k - 1, :, tile_at(t)],
            send_sem=p_ss.at[k - 1, t], recv_sem=p_rs.at[k - 1, t],
            device_id={"col": col_at(k)}, device_id_type=MESH,
        )

    p_shares = []
    for t in range(tiles):
        v = nn(win_t, z[:, tile_at(t)])
        sig = 0.5 * jnp.tanh(0.5 * v) + 0.5
        h = (v * sig).astype(BF16)
        p = nn(out_t, h)
        for c in range(cols_n):
            part[c, :, tile_at(t)] = p[c * cc:(c + 1) * cc]
            part_out[c, :, tile_at(t)] = p[c * cc:(c + 1) * cc].astype(wire)
        for k in range(1, cols_n):
            p_shares.append(p_share(k, t))
            p_shares[-1].start()
        if t == 0:
            for k in range(1, cols_n):
                g_arrives(k).wait_recv()
        g = g2[:, :, tile_at(t)].reshape(cols_n * cc, tile).astype(BF16)
        second_ref[...] += nt(g, h)
        ds = (nn(my_out, g) * (sig * (1.0 + v * (1.0 - sig)))).astype(BF16)
        first_ref[...] += nt(z[:, tile_at(t)], ds)

    if reduce_here:
        fr = first_ref.shape[0] // rows_n
        sr = second_ref.shape[0] // rows_n
        for j in range(rows_n):
            mine = [first_ref[j * fr:(j + 1) * fr], second_ref[j * sr:(j + 1) * sr]]
            if red.shape[1] > fr + sr:
                mine.append(jnp.zeros((red.shape[1] - fr - sr, hidden), F32))
            red[j] = jnp.concatenate(mine, 0).astype(red.dtype)

        def red_copy(k):
            return pltpu.make_async_remote_copy(
                src_ref=red.at[row_at(k)], dst_ref=red_in.at[k - 1],
                send_sem=red_ss.at[k - 1], recv_sem=red_rs.at[k - 1],
                device_id={"row": row_at(k)}, device_id_type=MESH,
            )

        def all_copy(k, slot):
            return pltpu.make_async_remote_copy(
                src_ref=summed.at[me], dst_ref=summed.at[slot],
                send_sem=all_ss.at[k - 1], recv_sem=all_rs.at[k - 1],
                device_id={"row": row_at(k)}, device_id_type=MESH,
            )

        def over_peers(body):
            lax.fori_loop(1, rows_n, lambda k, c: (body(k), c)[1], 0, unroll=5)

        over_peers(lambda k: red_copy(k).start())

    for copy in p_shares:
        copy.wait_recv()

    def class_block(r, carry):
        total = part[mc, :, lanes(r)]
        for k in range(cols_n - 1):
            total += part_in[k, :, lanes(r)].astype(F32)
        cls[r] = total.astype(BF16).astype(wire)
        return carry

    lax.fori_loop(0, nb, class_block, 0, unroll=4)

    for pos in range(6):
        for rank in range(2):
            cs[pos, rank] = cls[served[pos][rank]]
    cs[BEFORE, 2] = cls[nb - 1]
    cs[BEYOND, 2] = cls[0]
    c_copies = [swap(cs, cr, c_ss, c_rs, pos, row_at(-d)) for pos, d in enumerate(DISTANCES)]
    for copy in c_copies:
        copy.start()

    def s_band(r):
        values = jnp.concatenate([cls[r - 1], cls[r], cls[r + 1]], 1).astype(BF16)
        blocks = jnp.concatenate([band_ref[r, 0], band_ref[r, 1], band_ref[r, 2]], 1)
        gacc[r] = nt(values, blocks)

    inner(s_band)
    gacc[0] = nt(cls[0].astype(BF16), band_ref[0, 1]) + nt(cls[1].astype(BF16), band_ref[0, 2])
    gacc[last] = nt(cls[last - 1].astype(BF16), band_ref[last, 0]) + nt(cls[last].astype(BF16), band_ref[last, 1])

    if reduce_here:
        over_peers(lambda k: red_copy(k).wait_recv())
        total = red[me].astype(F32)
        for k in range(rows_n - 1):
            total += red_in[k].astype(F32)
        summed[me] = total.astype(summed.dtype)
        over_peers(lambda k: all_copy(k, me).start())

    for copy in c_copies:
        copy.wait_recv()
    for pos in range(6):
        for rank in range(2):
            s, row, live = read[pos][rank]
            contrib[2 * pos + rank, 0:cc] = nt(cr[pos, rank].astype(BF16), long_ref[s])
    gacc[0] += nt(cr[BEFORE, 2].astype(BF16), band_ref[0, 0])
    gacc[nb - 1] += nt(cr[BEYOND, 2].astype(BF16), band_ref[nb - 1, 2])

    def s_long(r, carry):
        total = gacc[r]
        for pos in range(6):
            for rank in range(2):
                s, row, live = read[pos][rank]
                total += (live * (row == r).astype(F32)) * contrib[2 * pos + rank, 0:cc]
        scores_ref[:, lanes(r)] = total.astype(BF16)
        return carry

    lax.fori_loop(0, nb, s_long, 0, unroll=4)

    results = [
        pltpu.make_async_copy(src, dst, out_sem.at[i])
        for i, (src, dst) in enumerate(((scores_ref, scores_hbm), (first_ref, first_hbm), (second_ref, second_hbm)))
    ]
    results[0].start()
    if reduce_here:
        over_peers(lambda k: all_copy(k, row_at(-k)).wait_recv())
        for j in range(rows_n):
            final = summed[j].astype(F32)
            first_ref[j * fr:(j + 1) * fr] = final[0:fr]
            second_ref[j * sr:(j + 1) * sr] = final[fr:fr + sr]
    results[1].start()
    results[2].start()
    if reduce_here:
        over_peers(lambda k: red_copy(k).wait_send())
        over_peers(lambda k: all_copy(k, me).wait_send())

    for copy in x_copies + g_copies + c_copies + g_shares + p_shares:
        copy.wait_send()
    for copy in results:
        copy.wait()


def hand_over(a, b, c, a_out, b_out, c_out, a_held, b_held, c_held, sem_in, sem_out):
    held = (a_held, b_held, c_held)
    arriving = [pltpu.make_async_copy(src, dst, sem_in.at[i]) for i, (src, dst) in enumerate(zip((a, b, c), held))]
    leaving = [
        pltpu.make_async_copy(src, dst, sem_out.at[i]) for i, (src, dst) in enumerate(zip(held, (a_out, b_out, c_out)))
    ]
    for copy in arriving:
        copy.start()
    for before, after in zip(arriving, leaving):
        before.wait()
        after.start()
    for copy in leaving:
        copy.wait()


def local(
    features, weight_in, weight_out, score_grad, band_blocks, long_blocks, long_rows, long_sources, long_counts,
):
    rows_n = lax.axis_size("row")
    cols_n = lax.axis_size("col")
    feats, nodes = features.shape
    nb = nodes // BLK
    hidden = weight_in.shape[1]
    cc = score_grad.shape[0]
    classes = weight_out.shape[1]
    wire = BF16 if cc % 16 == 0 else F32
    reduce_here = feats % (8 * rows_n) == 0 and classes % rows_n == 0 and hidden % BLK == 0
    chunk = -(-((feats + classes) // rows_n) // 16) * 16 if reduce_here else 16
    slices = rows_n if reduce_here else 1
    peers = max(slices - 1, 1)
    dma = pltpu.SemaphoreType.DMA
    hbm = pl.BlockSpec(memory_space=pl.ANY)
    scores, first, second = pl.pallas_call(
        functools.partial(kernel, rows_n, cols_n, reduce_here),
        out_shape=(
            jax.ShapeDtypeStruct((cc, nodes), BF16),
            jax.ShapeDtypeStruct((feats, hidden), F32),
            jax.ShapeDtypeStruct((classes, hidden), F32),
        ),
        in_specs=[hbm] * 9,
        out_specs=(hbm, hbm, hbm),
        scratch_shapes=[
            pltpu.VMEM((cc, nodes), BF16),
            pltpu.VMEM((feats, hidden), F32),
            pltpu.VMEM((classes, hidden), F32),
            dma((3,)),
            pltpu.VMEM(features.shape, BF16),
            pltpu.VMEM(weight_in.shape, BF16),
            pltpu.VMEM(weight_out.shape[::-1], BF16),
            pltpu.VMEM(score_grad.shape, BF16),
            pltpu.VMEM(band_blocks.shape, BF16),
            pltpu.VMEM(long_blocks.shape, BF16),
            pltpu.SMEM(long_rows.shape, jnp.int32),
            pltpu.SMEM(long_sources.shape, jnp.int32),
            pltpu.SMEM(long_counts.shape, jnp.int32),
            dma((9,)),
            pltpu.VMEM((nb, feats, BLK), BF16),
            pltpu.VMEM((nb, cc, BLK), wire),
            pltpu.VMEM((6, 3, feats, BLK), BF16),
            pltpu.VMEM((6, 3, feats, BLK), BF16),
            pltpu.VMEM((6, 3, cc, BLK), wire),
            pltpu.VMEM((6, 3, cc, BLK), wire),
            pltpu.VMEM((6, 3, cc, BLK), wire),
            pltpu.VMEM((6, 3, cc, BLK), wire),
            pltpu.VMEM((nb, feats, BLK), F32),
            pltpu.VMEM((SLOTS, feats, BLK), F32),
            pltpu.VMEM((feats, nodes), BF16),
            pltpu.VMEM((nb, cc, BLK), F32),
            pltpu.VMEM((cols_n, cc, nodes), wire),
            pltpu.VMEM((cols_n, cc, nodes), F32),
            pltpu.VMEM((cols_n, cc, nodes), wire),
            pltpu.VMEM((cols_n - 1, cc, nodes), wire),
            pltpu.VMEM((nb, cc, BLK), wire),
            pltpu.VMEM((slices, chunk, hidden), BF16),
            pltpu.VMEM((peers, chunk, hidden), BF16),
            pltpu.VMEM((slices, chunk, hidden), BF16),
            dma((6,)), dma((6,)), dma((6,)), dma((6,)), dma((6,)), dma((6,)),
            dma((cols_n - 1,)), dma((cols_n - 1,)), dma((cols_n - 1, nodes // (4 * BLK))), dma((cols_n - 1, nodes // (4 * BLK))),
            dma((peers,)), dma((peers,)), dma((peers,)), dma((peers,)),
        ],
        compiler_params=pltpu.CompilerParams(
            collective_id=0, has_side_effects=True, vmem_limit_bytes=VMEM_BYTES
        ),
    )(features, weight_in, weight_out.T, score_grad, band_blocks, long_blocks, long_rows, long_sources, long_counts)
    scores, first, second = pl.pallas_call(
        hand_over,
        out_shape=tuple(jax.ShapeDtypeStruct(a.shape, a.dtype) for a in (scores, first, second)),
        in_specs=[hbm] * 3,
        out_specs=(hbm, hbm, hbm),
        scratch_shapes=[pltpu.VMEM(a.shape, a.dtype) for a in (scores, first, second)] + [dma((3,)), dma((3,))],
        compiler_params=pltpu.CompilerParams(vmem_limit_bytes=VMEM_BYTES),
    )(scores, first, second)
    second = second.T
    if not reduce_here:
        first, second = lax.psum((first, second), "row")
    return scores, first, second


def solution(mesh):
    return jax.shard_map(
        local,
        mesh=mesh,
        in_specs=(
            P(None, "row"),
            P(None, "col"),
            P(),
            P("col", "row"),
            P("row", None, None, None),
            P("row", None, None),
            P("row", None),
            P(),
            P(),
        ),
        out_specs=(P("col", "row"), P(None, "col"), P("col", None)),
        check_vma=False,
    )
```

profile of v0, /device:TPU:0, one launch (start us, length us, event | category | flops | bytes accessed | tf_op | source)
XLA Modules:
  0.0 33.4 jit_solution(15724943379019707016)
XLA Ops:
  0.6 31.0 %shard_map.112 = (bf16[32,2048]{1,0:T(8,128)(2,1)}, f32[128,256]{1,0:T(8,128)}, f32[64,256]{1,0:T(8,128)}) custom-call(bf16[128,2048]{1,0:T(8,128)(2,1)} %x_hbm.1, bf16[128,256]{1,0:T(8,128)(2,1)} %win_hbm.1, bf16[64,512]{1,0:T(8,128)(2,1)} %bitcast.2, bf16[32,2048]{1,0:T(8,128)(2,1)} %sg_hbm.1, bf16[16,3,128,128]{3,2,1,0:T(8,128)(2,1)} %band_hbm.1, ...), custom_call_target="tpu_custom_call" | custom-call | tf_op jit(solution)/shard_map/pallas_call | solution.py:412
  31.7 1.7 %shard_map.113 = (bf16[32,2048]{1,0:T(8,128)(2,1)}, f32[128,256]{1,0:T(8,128)}, f32[64,256]{1,0:T(8,128)}) custom-call(bf16[32,2048]{1,0:T(8,128)(2,1)} %get-tuple-element.9.a, f32[128,256]{1,0:T(8,128)} %get-tuple-element.10.b, f32[64,256]{1,0:T(8,128)} %get-tuple-element.11.c), custom_call_target="tpu_custom_call" | custom-call | tf_op jit(solution)/shard_map/pallas_call | solution.py:464
where the time goes:
time: 33.5 us; the launch traced here: 33.4 us
  Pallas kernels  32.7 us (98%)
  between operations  0.64 us (2%)
    pallas_call x1, Pallas kernels, local(): pl.pallas_call(functools.partial(kernel, rows_n, cols_n, reduce_here), ou...  31 us
    pallas_call x1, Pallas kernels, local(): pl.pallas_call(hand_over, out_shape=tuple((jax.ShapeDtypeStruct(a.shape,...  1.69 us

commit v1 on v0

--- a/solution.py
+++ b/solution.py
@@ -43,7 +43,7 @@
     scores_hbm, first_hbm, second_hbm,
     scores_ref, first_ref, second_ref, out_sem,
     x_ref, win_ref, wout_ref, sg_ref, band_ref, long_ref, rows_ref, src_ref, count_ref, in_sem,
-    xb, sb, xs, xr, gs, gr, cs, cr, zacc, contrib, z, gacc, g2, part, part_out, part_in, cls, red, red_in, summed,
+    xb, sb, xs, xr, gs, gr, cs, cr, zacc, contrib, z, gacc, g2, act, slope, part, part_out, part_in, cls, red, red_in, summed,
     x_ss, x_rs, g_ss, g_rs, c_ss, c_rs, gc_ss, gc_rs, p_ss, p_rs, red_ss, red_rs, all_ss, all_rs,
 ):
     me = lax.axis_index("row")
@@ -109,7 +109,31 @@
             for s in slots_of(my_owners, row_at(d))
         ])
 
-    for copy in operands[3:5]:
+    operands[5].wait()
+    for r in range(nb):
+        xb[r] = x_ref[:, lanes(r)]
+    for pos in range(6):
+        for rank in range(2):
+            xs[pos, rank] = xb[served[pos][rank]]
+    xs[BEFORE, 2] = xb[nb - 1]
+    xs[BEYOND, 2] = xb[0]
+
+    pl.semaphore_wait(barrier, expected)
+
+    def swap(src, dst, ss, rs, pos, to):
+        span = pl.ds(0, blocks_sent(pos))
+        return pltpu.make_async_remote_copy(
+            src_ref=src.at[pos, span], dst_ref=dst.at[pos, span],
+            send_sem=ss.at[pos], recv_sem=rs.at[pos],
+            device_id={"row": to}, device_id_type=MESH,
+        )
+
+    g_copies = [swap(gs, gr, g_ss, g_rs, pos, row_at(d)) for pos, d in enumerate(DISTANCES)]
+    x_copies = [swap(xs, xr, x_ss, x_rs, pos, row_at(-d)) for pos, d in enumerate(DISTANCES)]
+    for pos in reversed(NEAR_FIRST):
+        x_copies[pos].start()
+
+    for copy in operands[3:5] + operands[6:7]:
         copy.wait()
     for r in range(nb):
         sb[r] = sg_ref[:, lanes(r)].astype(wire)
@@ -117,33 +141,10 @@
         for rank in range(2):
             s, row, live = read[pos][rank]
             gs[pos, rank] = (live * nn(sb[row].astype(BF16), long_ref[s])).astype(wire)
-    for copy in operands[5:7]:
-        copy.wait()
     gs[BEFORE, 2] = nn(sg_ref[:, lanes(0)], band_ref[0, 0]).astype(wire)
     gs[BEYOND, 2] = nn(sg_ref[:, lanes(nb - 1)], band_ref[nb - 1, 2]).astype(wire)
-    for r in range(nb):
-        xb[r] = x_ref[:, lanes(r)]
-    for pos in range(6):
-        for rank in range(2):
-            xs[pos, rank] = xb[served[pos][rank]]
-    xs[BEFORE, 2] = xb[nb - 1]
-    xs[BEYOND, 2] = xb[0]
-
-    pl.semaphore_wait(barrier, expected)
-
-    def swap(src, dst, ss, rs, pos, to):
-        span = pl.ds(0, blocks_sent(pos))
-        return pltpu.make_async_remote_copy(
-            src_ref=src.at[pos, span], dst_ref=dst.at[pos, span],
-            send_sem=ss.at[pos], recv_sem=rs.at[pos],
-            device_id={"row": to}, device_id_type=MESH,
-        )
-
-    g_copies = [swap(gs, gr, g_ss, g_rs, pos, row_at(d)) for pos, d in enumerate(DISTANCES)]
-    x_copies = [swap(xs, xr, x_ss, x_rs, pos, row_at(-d)) for pos, d in enumerate(DISTANCES)]
-    for copies in (g_copies, x_copies):
-        for pos in reversed(NEAR_FIRST):
-            copies[pos].start()
+    for pos in reversed(NEAR_FIRST):
+        g_copies[pos].start()
 
     def three(r):
         start = (r - 1) * BLK
@@ -260,12 +261,16 @@
         for k in range(1, cols_n):
             p_shares.append(p_share(k, t))
             p_shares[-1].start()
-        if t == 0:
-            for k in range(1, cols_n):
-                g_arrives(k).wait_recv()
+        act[:, tile_at(t)] = h
+        slope[:, tile_at(t)] = sig * (1.0 + v * (1.0 - sig))
+
+    for k in range(1, cols_n):
+        g_arrives(k).wait_recv()
+    for t in range(tiles):
+        h = act[:, tile_at(t)]
         g = g2[:, :, tile_at(t)].reshape(cols_n * cc, tile).astype(BF16)
         second_ref[...] += nt(g, h)
-        ds = (nn(my_out, g) * (sig * (1.0 + v * (1.0 - sig)))).astype(BF16)
+        ds = (nn(my_out, g) * slope[:, tile_at(t)]).astype(BF16)
         first_ref[...] += nt(z[:, tile_at(t)], ds)
 
     if reduce_here:
@@ -446,6 +451,8 @@
             pltpu.VMEM((feats, nodes), BF16),
             pltpu.VMEM((nb, cc, BLK), F32),
             pltpu.VMEM((cols_n, cc, nodes), wire),
+            pltpu.VMEM((hidden, nodes), BF16),
+            pltpu.VMEM((hidden, nodes), F32),
             pltpu.VMEM((cols_n, cc, nodes), F32),
             pltpu.VMEM((cols_n, cc, nodes), wire),
             pltpu.VMEM((cols_n - 1, cc, nodes), wire),

time: 33.5 us -> 36 us (1.075)
  Pallas kernels: 32.7 us -> 35.2 us
    pallas_call x1, Pallas kernels: 31 us -> 33.5 us  [local(): pl.pallas_call(functools.partial(kernel, rows_n, cols_n, reduce_here), ou...]
where the time goes in v1:
time: 36 us; the launch traced here: 35.9 us
  Pallas kernels  35.2 us (98%)
  between operations  0.64 us (2%)
    pallas_call x1, Pallas kernels, local(): pl.pallas_call(functools.partial(kernel, rows_n, cols_n, reduce_here), ou...  33.5 us
    pallas_call x1, Pallas kernels, local(): pl.pallas_call(hand_over, out_shape=tuple((jax.ShapeDtypeStruct(a.shape,...  1.69 us

profile of v1, /device:TPU:0, one launch (start us, length us, event | category | flops | bytes accessed | tf_op | source)
XLA Modules:
  0.0 35.9 jit_solution(14158598994134501287)
XLA Ops:
  0.6 33.5 %shard_map.112 = (bf16[32,2048]{1,0:T(8,128)(2,1)}, f32[128,256]{1,0:T(8,128)}, f32[64,256]{1,0:T(8,128)}) custom-call(bf16[128,2048]{1,0:T(8,128)(2,1)} %x_hbm.1, bf16[128,256]{1,0:T(8,128)(2,1)} %win_hbm.1, bf16[64,512]{1,0:T(8,128)(2,1)} %bitcast.2, bf16[32,2048]{1,0:T(8,128)(2,1)} %sg_hbm.1, bf16[16,3,128,128]{3,2,1,0:T(8,128)(2,1)} %band_hbm.1, ...), custom_call_target="tpu_custom_call" | custom-call | tf_op jit(solution)/shard_map/pallas_call | solution.py:417
  34.2 1.7 %shard_map.113 = (bf16[32,2048]{1,0:T(8,128)(2,1)}, f32[128,256]{1,0:T(8,128)}, f32[64,256]{1,0:T(8,128)}) custom-call(bf16[32,2048]{1,0:T(8,128)(2,1)} %get-tuple-element.9.a, f32[128,256]{1,0:T(8,128)} %get-tuple-element.10.b, f32[64,256]{1,0:T(8,128)} %get-tuple-element.11.c), custom_call_target="tpu_custom_call" | custom-call | tf_op jit(solution)/shard_map/pallas_call | solution.py:471
